TPU v7x, 32 devices: a whole 2x2x4 slice. The times are simulated.
32 devices in a mesh: occ: 2 (over x), vir: 16 (over z, y, core).
Axes of the slice: x: 2, y: 2, z: 4, core: 2. Of those that a mesh axis runs over, the one named last changes fastest.
Arguments:
- amplitudes: bfloat16 [256, 240, 2112], P(('occ', 'vir')), may hold values from -6 to 6
- integrals: bfloat16 [240, 2112, 256], P('occ', 'vir'), may hold values from -0.01171875 to 0.01171875
- screen: int32 [5, 22], replicated, may hold values 0 or 1
- row_gap: float32 [256], P('occ'), may hold values from 0.2 to 2
- col_gap: float32 [256], P('vir'), may hold values from 0.2 to 2
Outputs:
- update: float32 [256, 256], P('occ', 'vir')
Inputs may be any that keep to these rules, and one draw needn't show every extreme that they name: `screen`: 1 keeps the amplitudes of an occupied tile and a virtual tile, 0 screens them out.
All inputs are finite; a program needn't handle non-finite values.
Results may differ from a plain program's by a relative error of at most 0.0003.
Values may be sent and summed in bfloat16 or wider, within the bound.
A program may use at most 128 MiB of HBM per device.

v0:
```python
import jax
import jax.numpy as jnp
from jax import lax
from jax.sharding import PartitionSpec as P


def shards(amplitudes, integrals, screen, row_gap, col_gap):
    rows_here, occ_all, vir_all = amplitudes.shape
    tiles_occ, tiles_vir = screen.shape
    keep_mask = jnp.broadcast_to(
        screen.astype(jnp.bfloat16)[:, None, :, None],
        (tiles_occ, occ_all // tiles_occ, tiles_vir, vir_all // tiles_vir),
    ).reshape(occ_all, vir_all)
    screened = amplitudes * keep_mask[None]
    occ_part, vir_part, col_total = integrals.shape
    relaid = lax.all_to_all(
        lax.all_to_all(screened[None, None], "occ", split_axis=3, concat_axis=0, tiled=True),
        "vir",
        split_axis=4,
        concat_axis=1,
        tiled=True,
    )
    flat_rows = relaid.reshape(-1, occ_part * vir_part)
    int_slab = integrals.reshape(occ_part * vir_part, col_total)
    per_vir = lax.psum_scatter(
        lax.dot_general(
            int_slab, flat_rows, (((0,), (1,)), ((), ())), preferred_element_type=jnp.float32
        ),
        "vir",
        scatter_dimension=0,
        tiled=True,
    )
    cycle_cols = lax.psum_scatter(per_vir, "occ", scatter_dimension=1, tiled=True)
    cycle_sum = cycle_cols.T
    update = cycle_sum / (row_gap[:, None] + col_gap[None, :])
    return update


def solution(mesh):
    placed = (P(("occ", "vir"), None, None), P("occ", "vir", None), P(), P("occ"), P("vir"))
    return jax.shard_map(
        shards, mesh=mesh, in_specs=placed, out_specs=P("occ", "vir"), check_vma=False
    )
```

profile of v0, /device:TPU:0, one launch (start us, length us, event | category | flops | bytes accessed | tf_op | source)
XLA Modules:
  0.0 464.6 jit_solution(2814639098561962855)
XLA Ops:
  6.5 0.7 convert_element_type.3
  7.2 0.3 broadcast_in_dim.4
  7.5 1.0 mul.10
  8.5 7.6 %fusion = bf16[1,1,8,240,2112]{4,2,1,0,3:T(8,128)(2,1)S(1)} fusion(bf16[8,240,2112]{2,1,0:T(8,128)(2,1)} %param.5, bf16[240,2112]{1,0:T(8,128)(2,1)S(1)} %mul.10), kind=kLoop, calls=%fused_computation.1 | loop fusion | flops 4055040 | bytes 17233920 | tf_op jit(solution)/shard_map/broadcast_in_dim | solution.py:17
  16.1 97.7 %all_to_all.33 = bf16[1,1,8,240,2112]{4,2,1,0,3:T(8,128)(2,1)} all-to-all(bf16[1,1,8,240,2112]{4,2,1,0,3:T(8,128)(2,1)S(1)} %fusion), channel_id=1, replica_groups=mesh['occ'=2,'vir'=16] {'occ'}, dimensions={3} | all-to-all | bytes 16220160 | tf_op jit(solution)/shard_map/all_to_all | solution.py:17
  113.9 7.6 %copy.22 = bf16[1,1,8,240,2112]{4,3,2,1,0:T(8,128)(2,1)} copy(bf16[1,1,8,240,2112]{4,2,1,0,3:T(8,128)(2,1)} %all_to_all.33) | data formatting | bytes 16220160 | tf_op jit(solution)/shard_map/all_to_all | solution.py:17
  121.5 22.5 %copy.23 = bf16[2,1,8,120,2112]{3,0,2,1,4:T(2,128)(2,1)} copy(bf16[2,1,8,120,2112]{4,3,0,2,1:T(8,128)(2,1)} %bitcast.22) | data formatting | bytes 16220160 | tf_op jit(solution)/shard_map/all_to_all | solution.py:17
  143.9 6.2 %all-to-all-start.1 = ((bf16[2,1,8,120,2112]{3,0,2,1,4:T(2,128)(2,1)}), bf16[2,1,8,120,2112]{3,0,2,1,4:T(2,128)(2,1)}, u32[]{:S(2)}, u32[]{:S(2)}) async-start(bf16[2,1,8,120,2112]{3,0,2,1,4:T(2,128)(2,1)} %copy.23), calls=%async_computation.1 | async-start | bytes 17301504 | tf_op jit(solution)/shard_map/all_to_all | solution.py:16
  150.2 0.0 reduce-scatter.7.cloned.1.call-start
  150.2 8.2 %copy.26 = bf16[120,132,256]{2,1,0:T(8,128)(2,1)} copy(bf16[120,132,256]{2,0,1:T(8,128)(2,1)} %param.6) | data formatting | bytes 16220160 | tf_op args[1]
  158.5 11.9 %reshape.12 = bf16[15840,256]{1,0:T(8,128)(2,1)} reshape(bf16[120,132,256]{2,1,0:T(8,128)(2,1)} %copy.26) | data formatting | bytes 16220160 | tf_op jit(solution)/shard_map/reshape | solution.py:24
  170.4 135.1 %all-to-all-done.1 = bf16[2,1,8,120,2112]{3,0,2,1,4:T(2,128)(2,1)} async-done(((bf16[2,1,8,120,2112]{3,0,2,1,4:T(2,128)(2,1)}), bf16[2,1,8,120,2112]{3,0,2,1,4:T(2,128)(2,1)}, u32[]{:S(2)}, u32[]{:S(2)}) %all-to-all-start.1) | async-done | bytes 8110112 | tf_op jit(solution)/shard_map/all_to_all | solution.py:16
  305.5 7.9 %copy.24 = bf16[2,1,8,120,2112]{3,2,4,0,1:T(8,128)(2,1)} copy(bf16[2,1,8,120,2112]{3,0,2,1,4:T(2,128)(2,1)} %all-to-all-done.1) | data formatting | bytes 16220160 | tf_op jit(solution)/shard_map/all_to_all | solution.py:16
  313.4 15.9 %copy.25 = bf16[2,16,1,8,120,132]{5,4,3,1,0,2:T(8,128)(2,1)} copy(bf16[2,16,1,8,120,132]{4,3,5,1,0,2:T(8,128)(2,1)} %bitcast.21) | data formatting | bytes 16220160 | tf_op jit(solution)/shard_map/all_to_all | solution.py:16
  329.2 20.0 %reshape.11 = bf16[256,15840]{1,0:T(8,128)(2,1)} reshape(bf16[2,16,1,8,120,132]{5,4,3,1,0,2:T(8,128)(2,1)} %copy.25) | data formatting | bytes 16220160 | tf_op jit(solution)/shard_map/reshape | solution.py:23
  349.2 0.0 copy-start
  349.2 0.0 copy-start.1
  349.2 7.9 %convolution_bitcast_fusion = f32[256,256]{0,1:T(8,128)S(1)} fusion(bf16[256,15840]{1,0:T(8,128)(2,1)} %reshape.11, bf16[15840,256]{1,0:T(8,128)(2,1)} %reshape.12), kind=kOutput, calls=%fused_computation.2 | convolution fusion | flops 2076180480 | bytes 16482304 | tf_op jit(solution)/shard_map/dot_general | solution.py:26
  357.1 0.8 copy.28
  357.9 0.0 reduce-scatter.7.cloned.1.call-update
  357.9 0.0 reduce-scatter.5.cloned.1.call-start
  358.0 87.3 %reduce-scatter.7.cloned.1.call-done = f32[16,256]{1,0:T(8,128)} async-done(((f32[256,256]{1,0:T(8,128)}), f32[16,256]{1,0:T(8,128)}) %reduce-scatter.7.cloned.1.call-update) | async-done | bytes 16400 | tf_op jit(solution)/shard_map/reduce_scatter | solution.py:25
  445.3 0.0 reduce-scatter.5.cloned.1.call-update
  445.3 11.0 %reduce-scatter.5.cloned.1.call-done = f32[16,128]{1,0:T(8,128)} async-done(((f32[16,256]{1,0:T(8,128)}), f32[16,128]{1,0:T(8,128)}) %reduce-scatter.5.cloned.1.call-update) | async-done | bytes 8208 | tf_op jit(solution)/shard_map/reduce_scatter | solution.py:33
  456.3 0.0 copy-done
  456.3 0.0 copy-done.1
  456.3 1.4 bitcast_divide_fusion
Async XLA Ops:
  143.9 161.5 %all-to-all-start.1 = ((bf16[2,1,8,120,2112]{3,0,2,1,4:T(2,128)(2,1)}), bf16[2,1,8,120,2112]{3,0,2,1,4:T(2,128)(2,1)}, u32[]{:S(2)}, u32[]{:S(2)}) async-start(bf16[2,1,8,120,2112]{3,0,2,1,4:T(2,128)(2,1)} %copy.23), calls=%async_computation.1 | async-start | bytes 17301504 | tf_op jit(solution)/shard_map/all_to_all | solution.py:16
  150.2 295.1 %reduce-scatter.7.cloned.1.call-start = ((), (), s32[]{:S(2)}) async-start(), calls=%async_computation.5 | async-start | bytes 278528 | tf_op jit(solution)/shard_map/reduce_scatter | solution.py:25
  349.2 107.2 %copy-start = (f32[16]{0:T(128)S(1)}, f32[16]{0:T(128)}, u32[]{:S(2)}) copy-start(f32[16]{0:T(128)} %param.9) | copy-start | bytes 196
  349.2 107.2 %copy-start.1 = (f32[128]{0:T(128)S(1)}, f32[128]{0:T(128)}, u32[]{:S(2)}) copy-start(f32[128]{0:T(128)} %param.8) | copy-start | bytes 1540
  357.9 98.4 %reduce-scatter.5.cloned.1.call-start = ((), (), s32[]{:S(2)}) async-start(), calls=%async_computation.4 | async-start | bytes 24576 | tf_op jit(solution)/shard_map/reduce_scatter | solution.py:33
Sparse Core Ops, SparseCore 0:
  358.1 87.2 reduce-scatter.6
  447.5 8.7 reduce-scatter.4
where the time goes:
time: 467 us; the launch traced here: 465 us
  waiting for transfers between devices  233 us (50%)
  blocking collectives  97.7 us (21%)
  local copies, waits for them, and re-layouts  96.1 us (21%)
  between operations  13.5 us (3%)
  other arithmetic  9.62 us (2%)
  matrix products  7.89 us (2%)
  starting transfers between devices  6.32 us (1%)
    all_to_all x1, waiting for transfers between devices, shards(): lax.all_to_all(lax.all_to_all(screened[None, None], 'occ', split_axis=3,...  135 us
    all_to_all x1, blocking collectives, shards(): lax.all_to_all(screened[None, None], 'occ', split_axis=3, concat_axis=0,...  97.7 us
    reduce_scatter x1, waiting for transfers between devices, shards(): lax.psum_scatter(lax.dot_general(int_slab, flat_rows, (((0,), (1,)), ((),...  87.3 us
    all_to_all x2, local copies, waits for them, and re-layouts, shards(): lax.all_to_all(screened[None, None], 'occ', split_axis=3, concat_axis=0,...  30.1 us
    all_to_all x2, local copies, waits for them, and re-layouts, shards(): lax.all_to_all(lax.all_to_all(screened[None, None], 'occ', split_axis=3,...  23.7 us
    reshape x1, local copies, waits for them, and re-layouts, shards(): flat_rows = relaid.reshape(-1, occ_part * vir_part)  20 us
    reshape x1, local copies, waits for them, and re-layouts, shards(): int_slab = integrals.reshape(occ_part * vir_part, col_total)  11.9 us
    reduce_scatter x1, waiting for transfers between devices, shards(): lax.psum_scatter(per_vir, 'occ', scatter_dimension=1, tiled=True)  11 us
  transfers between devices with their start and end apart: 3, of which 3 were waited for; matrix products, arithmetic and copies ran while one was open for 4% of the time, Pallas kernels for 0%

commit v1 on v0

v1 whole, which is shorter than its diff:
```python
import functools

import jax
import jax.numpy as jnp
from jax import lax
from jax.experimental import pallas as pl
from jax.experimental.pallas import tpu as pltpu
from jax.sharding import PartitionSpec as P

MESH = pl.DeviceIdType.MESH


def keep_mask(screen, occ_all, vir_all):
    tiles_occ, tiles_vir = screen.shape
    return jnp.broadcast_to(
        screen.astype(jnp.bfloat16)[:, None, :, None],
        (tiles_occ, occ_all // tiles_occ, tiles_vir, vir_all // tiles_vir),
    ).reshape(occ_all, vir_all)


def plain_shards(amplitudes, integrals, screen, row_gap, col_gap):
    occ_all, vir_all = amplitudes.shape[1:]
    screened = amplitudes * keep_mask(screen, occ_all, vir_all)[None]
    occ_part, vir_part, col_total = integrals.shape
    relaid = lax.all_to_all(
        lax.all_to_all(screened[None, None], "occ", split_axis=3, concat_axis=0, tiled=True),
        "vir",
        split_axis=4,
        concat_axis=1,
        tiled=True,
    )
    flat_rows = relaid.reshape(-1, occ_part * vir_part)
    int_slab = integrals.reshape(occ_part * vir_part, col_total)
    per_vir = lax.psum_scatter(
        lax.dot_general(
            int_slab, flat_rows, (((0,), (1,)), ((), ())), preferred_element_type=jnp.float32
        ),
        "vir",
        scatter_dimension=0,
        tiled=True,
    )
    cycle_cols = lax.psum_scatter(per_vir, "occ", scatter_dimension=1, tiled=True)
    return cycle_cols.T / (row_gap[:, None] + col_gap[None, :])


def kernel(
    n_occ, n_vir, group,
    send_ref, int_ref, row_ref, col_ref, out_ref,
    recv, ints, acc, parts, red,
    int_sem, own_sem, send_sems, recv_sems, psend_sems, precv_sems,
):
    n = n_occ * n_vir
    my_occ, my_vir = lax.axis_index("occ"), lax.axis_index("vir")
    me = my_occ * n_vir + my_vir
    vir_part, rows_here = recv.shape[1:3]
    cols_here, rows_out = red.shape[1:]

    load = pltpu.make_async_copy(int_ref, ints, int_sem)
    load.start()

    def target(step):
        to = lax.rem(me + step, n)
        return to // n_vir, lax.rem(to, n_vir)

    barrier = pltpu.get_barrier_semaphore()

    def greet(step, carry):
        pl.semaphore_signal(barrier, inc=1, device_id=target(step), device_id_type=MESH)
        return carry

    lax.fori_loop(1, n, greet, 0)
    pl.semaphore_wait(barrier, n - 1)

    def block(step):
        to_occ, to_vir = target(step)
        return pltpu.make_async_remote_copy(
            src_ref=send_ref.at[to_occ, pl.ds(to_vir * vir_part, vir_part)],
            dst_ref=recv.at[step],
            send_sem=send_sems.at[step],
            recv_sem=recv_sems.at[step],
            device_id=(to_occ, to_vir),
            device_id_type=MESH,
        )

    def send_block(step, carry):
        block(step).start()
        return carry

    lax.fori_loop(1, n, send_block, 0)
    own = pltpu.make_async_copy(
        send_ref.at[my_occ, pl.ds(my_vir * vir_part, vir_part)], recv.at[0], own_sem
    )
    own.start()
    load.wait()
    own.wait()

    for first in range(0, n, group):
        def arrive(step, carry):
            block(step).wait_recv()
            return carry

        lax.fori_loop(max(first, 1), first + group, arrive, 0)

        def multiply(c, total):
            left = recv[first:first + group, c].astype(jnp.float32)
            left = left.reshape(group * rows_here, left.shape[-1]).astype(jnp.bfloat16)
            return total + jnp.dot(left, ints[c], preferred_element_type=jnp.float32)

        total = lax.fori_loop(
            0, vir_part, multiply,
            jnp.zeros((group * rows_here, ints.shape[-1]), jnp.float32),
        )
        for place in range(group):
            origin = lax.rem(me + n - (first + place), n)
            acc[pl.ds(pl.multiple_of(origin * rows_here, rows_here), rows_here), :] = total[
                place * rows_here:(place + 1) * rows_here
            ]

    for half in range(n_occ):
        parts[half] = acc[half * rows_out:(half + 1) * rows_out, :].T

    def piece(step):
        to_occ, to_vir = target(step)
        return pltpu.make_async_remote_copy(
            src_ref=parts.at[
                to_occ, pl.ds(pl.multiple_of(to_vir * cols_here, cols_here), cols_here)
            ],
            dst_ref=red.at[step],
            send_sem=psend_sems.at[step],
            recv_sem=precv_sems.at[step],
            device_id=(to_occ, to_vir),
            device_id_type=MESH,
        )

    def send_piece(step, carry):
        piece(step).start()
        return carry

    lax.fori_loop(1, n, send_piece, 0)

    def add_piece(step, total):
        piece(step).wait_recv()
        return total + red[step]

    mine = parts[my_occ, pl.ds(pl.multiple_of(my_vir * cols_here, cols_here), cols_here), :]
    total = lax.fori_loop(1, n, add_piece, mine)
    out_ref[...] = total / (row_ref[...] + col_ref[...])

    def drain(step, carry):
        block(step).wait_send()
        piece(step).wait_send()
        return carry

    lax.fori_loop(1, n, drain, 0)


def kernel_shards(n_occ, n_vir, amplitudes, integrals, screen, row_gap, col_gap):
    rows_here, occ_all, vir_all = amplitudes.shape
    occ_part, vir_part, col_total = integrals.shape
    n = n_occ * n_vir
    rows_out, cols_here = row_gap.shape[0], col_gap.shape[0]
    screened = amplitudes * keep_mask(screen, occ_all, vir_all)[None]
    send = jnp.transpose(
        screened.reshape(rows_here, n_occ, occ_part, vir_all), (1, 3, 0, 2)
    )
    ints = jnp.transpose(integrals, (1, 0, 2))
    vmem = pl.BlockSpec(memory_space=pltpu.VMEM)
    anywhere = pl.BlockSpec(memory_space=pl.ANY)
    dma = pltpu.SemaphoreType.DMA
    out = pl.pallas_call(
        functools.partial(kernel, n_occ, n_vir, 8),
        out_shape=jax.ShapeDtypeStruct((cols_here, rows_out), jnp.float32),
        in_specs=[anywhere, anywhere, vmem, vmem],
        out_specs=vmem,
        scratch_shapes=[
            pltpu.VMEM((n, vir_part, rows_here, occ_part), jnp.bfloat16),
            pltpu.VMEM((vir_part, occ_part, col_total), jnp.bfloat16),
            pltpu.VMEM((n * rows_here, col_total), jnp.float32),
            pltpu.VMEM((n_occ, col_total, rows_out), jnp.float32),
            pltpu.VMEM((n, cols_here, rows_out), jnp.float32),
            dma, dma, dma((n,)), dma((n,)), dma((n,)), dma((n,)),
        ],
        compiler_params=pltpu.CompilerParams(
            collective_id=0, has_side_effects=True, vmem_limit_bytes=48 * 2**20
        ),
    )(send, ints, row_gap.reshape(1, rows_out), col_gap.reshape(cols_here, 1))
    return out.T


def solution(mesh):
    n_occ, n_vir = mesh.shape["occ"], mesh.shape["vir"]

    def shards(amplitudes, integrals, screen, row_gap, col_gap):
        fits = (
            amplitudes.shape[0] % 8 == 0
            and row_gap.shape[0] % 128 == 0
            and col_gap.shape[0] % 8 == 0
            and (n_occ * n_vir) % 8 == 0
        )
        if fits:
            return kernel_shards(n_occ, n_vir, amplitudes, integrals, screen, row_gap, col_gap)
        return plain_shards(amplitudes, integrals, screen, row_gap, col_gap)

    placed = (P(("occ", "vir"), None, None), P("occ", "vir", None), P(), P("occ"), P("vir"))
    return jax.shard_map(
        shards, mesh=mesh, in_specs=placed, out_specs=P("occ", "vir"), check_vma=False
    )
```

time: 467 us -> 267 us (0.57)
  Pallas kernels: 0 us -> 244 us
  waiting for transfers between devices: 233 us -> 0 us
  blocking collectives: 97.7 us -> 0 us
  local copies, waits for them, and re-layouts: 96.1 us -> 14.5 us
  between operations: 13.5 us -> 0.03 us
  matrix products: 7.89 us -> 0 us
  starting transfers between devices: 6.32 us -> 0 us
    pallas_call x0 -> x1, Pallas kernels: none -> 244 us  [kernel_shards(): pl.pallas_call(functools.partial(kernel, n_occ, n_vir, 8), out_shape=jax....]
    all_to_all x1 -> x0, waiting for transfers between devices: 135 us -> none  [shards(): lax.all_to_all(lax.all_to_all(screened[None, None], 'occ', split_axis=3,...]
    reduce_scatter x2 -> x0, waiting for transfers between devices: 98.3 us -> none  [the longest x1 87.3 us: shards(): lax.psum_scatter(lax.dot_general(int_slab, flat_rows, (((0,), (1,)), ((),...]
    all_to_all x1 -> x0, blocking collectives: 97.7 us -> none  [shards(): lax.all_to_all(screened[None, None], 'occ', split_axis=3, concat_axis=0,...]
    all_to_all x4 -> x0, local copies, waits for them, and re-layouts: 53.8 us -> none  [the longest x2 30.1 us: shards(): lax.all_to_all(screened[None, None], 'occ', split_axis=3, concat_axis=0,...]
    reshape x2, local copies, waits for them, and re-layouts: 31.9 us -> 12.6 us  [the longest x1 12.5 us: kernel_shards(): screened.reshape(rows_here, n_occ, occ_part, vir_all)]
    unnamed x6 -> x5, local copies, waits for them, and re-layouts: 9.05 us -> 0.61 us
    dot_general x1 -> x0, matrix products: 7.89 us -> none  [shards(): lax.dot_general(int_slab, flat_rows, (((0,), (1,)), ((), ())), preferred_...]
  transfers between devices with their start and end apart: 3 -> 0, of which waited for: 3 -> 0; matrix products, arithmetic and copies ran while one was open for 4% -> 0% of each run, Pallas kernels for 0% -> 0%
where the time goes in v1:
time: 267 us
  Pallas kernels  244 us (91%)
  local copies, waits for them, and re-layouts  14.5 us (5%)
  other arithmetic  8.16 us (3%)
    pallas_call x1, Pallas kernels, kernel_shards(): pl.pallas_call(functools.partial(kernel, n_occ, n_vir, 8), out_shape=jax....  244 us
    reshape x1, local copies, waits for them, and re-layouts, kernel_shards(): screened.reshape(rows_here, n_occ, occ_part, vir_all)  12.5 us
    mul x1, other arithmetic, kernel_shards(): screened = amplitudes * keep_mask(screen, occ_all, vir_all)[None]  7.47 us

profile of v1, /device:TPU:0, one launch (start us, length us, event | category | flops | bytes accessed | tf_op | source)
XLA Modules:
  0.0 266.5 jit_solution(16667617086609479708)
XLA Ops:
  0.0 0.7 convert_element_type.3
  0.7 0.3 broadcast_in_dim.2
  1.0 1.0 mul.10
  2.0 7.5 %broadcast_multiply_fusion = bf16[8,240,2112]{2,1,0:T(8,128)(2,1)} fusion(bf16[8,240,2112]{2,1,0:T(8,128)(2,1)} %param.5, bf16[240,2112]{1,0:T(8,128)(2,1)S(1)} %mul.10), kind=kLoop, calls=%fused_computation | loop fusion | flops 4055040 | bytes 17233920 | tf_op jit(solution)/shard_map/mul | solution.py:162
  9.5 0.0 copy-start.1
  9.5 0.0 copy-start
  9.5 12.5 %copy.7 = bf16[8,2,120,2112]{2,0,3,1:T(8,128)(2,1)} copy(bf16[8,2,120,2112]{3,2,1,0:T(8,128)(2,1)} %bitcast.9) | data formatting | bytes 16220160 | tf_op jit(solution)/shard_map/reshape | solution.py:164
  22.0 0.0 copy-done.1
  22.0 0.1 copy.8.col_ref
  22.1 0.0 copy-done
  22.1 243.8 %shard_map.55 = f32[16,128]{1,0:T(8,128)S(1)} custom-call(bf16[2,2112,8,120]{3,2,1,0:T(8,128)(2,1)} %bitcast.8, bf16[132,120,256]{2,1,0:T(8,128)(2,1)} %bitcast.10, f32[1,128]{1,0:T(1,128)S(1)} %bitcast.7, f32[16,1]{1,0:T(8,128)S(1)} %copy.8.col_ref), custom_call_target="tpu_custom_call" | custom-call | tf_op jit(solution)/shard_map/pallas_call | solution.py:170
  265.9 0.6 copy.10
Async XLA Ops:
  9.5 12.5 %copy-start.1 = (f32[16]{0:T(128)S(1)}, f32[16]{0:T(128)}, u32[]{:S(2)}) copy-start(f32[16]{0:T(128)} %param.9) | copy-start | bytes 196
  9.5 12.6 %copy-start = (f32[128]{0:T(128)S(1)}, f32[128]{0:T(128)}, u32[]{:S(2)}) copy-start(f32[128]{0:T(128)} %param.8) | copy-start | bytes 1540

commit v2 on v1

--- a/solution.py
+++ b/solution.py
@@ -45,21 +45,45 @@
 
 def kernel(
     n_occ, n_vir, group,
-    send_ref, int_ref, row_ref, col_ref, out_ref,
+    send_ref, int_ref, screen_ref, row_ref, col_ref, out_ref,
     recv, ints, acc, parts, red,
     int_sem, own_sem, send_sems, recv_sems, psend_sems, precv_sems,
 ):
     n = n_occ * n_vir
     my_occ, my_vir = lax.axis_index("occ"), lax.axis_index("vir")
     me = my_occ * n_vir + my_vir
-    vir_part, rows_here = recv.shape[1:3]
+    vir_part, rows_here, occ_part = recv.shape[1:]
     cols_here, rows_out = red.shape[1:]
+
+    tiles_occ, tiles_vir = screen_ref.shape
+    tile_occ, tile_vir = occ_part * n_occ // tiles_occ, vir_part * n_vir // tiles_vir
+    occ_tile = (
+        lax.broadcasted_iota(jnp.int32, (1, occ_part), 1) + my_occ * occ_part
+    ) // tile_occ
+
+    def keep(c):
+        vir_tile = (my_vir * vir_part + c) // tile_vir
+        kept = jnp.zeros((1, occ_part), jnp.float32)
+        for t in range(tiles_occ):
+            flag = screen_ref[t, vir_tile].astype(jnp.float32)
+            kept = jnp.where(occ_tile == t, flag, kept)
+        return kept
 
     load = pltpu.make_async_copy(int_ref, ints, int_sem)
     load.start()
 
+    bits = n.bit_length() - 1
+    order = (0, 3, 4, 1, 2) if bits == 5 else tuple(range(bits))
+
+    def partner(step):
+        to = me
+        for place, bit in enumerate(order):
+            flip = lax.rem(step // 2**place, 2)
+            to = to + flip * (2**bit - 2 ** (bit + 1) * lax.rem(me // 2**bit, 2))
+        return to
+
     def target(step):
-        to = lax.rem(me + step, n)
+        to = partner(step)
         return to // n_vir, lax.rem(to, n_vir)
 
     barrier = pltpu.get_barrier_semaphore()
@@ -103,15 +127,17 @@
 
         def multiply(c, total):
             left = recv[first:first + group, c].astype(jnp.float32)
-            left = left.reshape(group * rows_here, left.shape[-1]).astype(jnp.bfloat16)
+            left = left.reshape(group * rows_here, occ_part) * keep(c)
+            left = left.astype(jnp.bfloat16)
             return total + jnp.dot(left, ints[c], preferred_element_type=jnp.float32)
 
         total = lax.fori_loop(
             0, vir_part, multiply,
             jnp.zeros((group * rows_here, ints.shape[-1]), jnp.float32),
+            unroll=4,
         )
         for place in range(group):
-            origin = lax.rem(me + n - (first + place), n)
+            origin = partner(first + place)
             acc[pl.ds(pl.multiple_of(origin * rows_here, rows_here), rows_here), :] = total[
                 place * rows_here:(place + 1) * rows_here
             ]
@@ -159,9 +185,8 @@
     occ_part, vir_part, col_total = integrals.shape
     n = n_occ * n_vir
     rows_out, cols_here = row_gap.shape[0], col_gap.shape[0]
-    screened = amplitudes * keep_mask(screen, occ_all, vir_all)[None]
     send = jnp.transpose(
-        screened.reshape(rows_here, n_occ, occ_part, vir_all), (1, 3, 0, 2)
+        amplitudes.reshape(rows_here, n_occ, occ_part, vir_all), (1, 3, 0, 2)
     )
     ints = jnp.transpose(integrals, (1, 0, 2))
     vmem = pl.BlockSpec(memory_space=pltpu.VMEM)
@@ -170,7 +195,9 @@
     out = pl.pallas_call(
         functools.partial(kernel, n_occ, n_vir, 8),
         out_shape=jax.ShapeDtypeStruct((cols_here, rows_out), jnp.float32),
-        in_specs=[anywhere, anywhere, vmem, vmem],
+        in_specs=[
+            anywhere, anywhere, pl.BlockSpec(memory_space=pltpu.SMEM), vmem, vmem
+        ],
         out_specs=vmem,
         scratch_shapes=[
             pltpu.VMEM((n, vir_part, rows_here, occ_part), jnp.bfloat16),
@@ -183,7 +210,7 @@
         compiler_params=pltpu.CompilerParams(
             collective_id=0, has_side_effects=True, vmem_limit_bytes=48 * 2**20
         ),
-    )(send, ints, row_gap.reshape(1, rows_out), col_gap.reshape(cols_here, 1))
+    )(send, ints, screen, row_gap.reshape(1, rows_out), col_gap.reshape(cols_here, 1))
     return out.T
 
 
@@ -196,6 +223,7 @@
             and row_gap.shape[0] % 128 == 0
             and col_gap.shape[0] % 8 == 0
             and (n_occ * n_vir) % 8 == 0
+            and (n_occ * n_vir).bit_count() == 1
         )
         if fits:
             return kernel_shards(n_occ, n_vir, amplitudes, integrals, screen, row_gap, col_gap)

time: 267 us -> 229 us (0.86)
  Pallas kernels: 244 us -> 215 us
  other arithmetic: 8.16 us -> 0 us
    pallas_call x1, Pallas kernels: 244 us -> 215 us  [kernel_shards(): pl.pallas_call(functools.partial(kernel, n_occ, n_vir, 8), out_shape=jax....]
    mul x1 -> x0, other arithmetic: 7.47 us -> none  [kernel_shards(): screened = amplitudes * keep_mask(screen, occ_all, vir_all)[None]]
where the time goes in v2:
time: 229 us
  Pallas kernels  215 us (94%)
  local copies, waits for them, and re-layouts  13.9 us (6%)
    pallas_call x1, Pallas kernels, kernel_shards(): pl.pallas_call(functools.partial(kernel, n_occ, n_vir, 8), out_shape=jax....  215 us
    reshape x1, local copies, waits for them, and re-layouts, kernel_shards(): amplitudes.reshape(rows_here, n_occ, occ_part, vir_all)  12.5 us

profile of v2, /device:TPU:0, one launch (start us, length us, event | category | flops | bytes accessed | tf_op | source)
XLA Modules:
  0.0 228.7 jit_solution(1453486374550209235)
XLA Ops:
  0.0 0.7 copy.8.col_ref
  0.7 0.0 copy-start
  0.7 0.0 copy-start.1
  0.7 12.5 %copy.7 = bf16[8,2,120,2112]{2,0,3,1:T(8,128)(2,1)} copy(bf16[8,2,120,2112]{3,2,1,0:T(8,128)(2,1)} %bitcast.9) | data formatting | bytes 16220160 | tf_op jit(solution)/shard_map/reshape | solution.py:189
  13.3 0.0 copy-done
  13.3 0.0 copy-done.1
  13.3 214.8 %shard_map.55 = f32[16,128]{1,0:T(8,128)S(1)} custom-call(bf16[2,2112,8,120]{3,2,1,0:T(8,128)(2,1)} %bitcast.8, bf16[132,120,256]{2,1,0:T(8,128)(2,1)} %bitcast.10, s32[5,22]{1,0:T(8,128)S(1)} %copy-done, f32[1,128]{1,0:T(1,128)S(1)} %bitcast.7, f32[16,1]{1,0:T(8,128)S(1)} %copy.8.col_ref), custom_call_target="tpu_custom_call" | custom-call | tf_op jit(solution)/shard_map/pallas_call | solution.py:195
  228.1 0.6 copy.10
Async XLA Ops:
  0.7 12.5 %copy-start = (s32[5,22]{1,0:T(8,128)S(1)}, s32[5,22]{1,0:T(8,128)}, u32[]{:S(2)}) copy-start(s32[5,22]{1,0:T(8,128)} %screen_ref.1) | copy-start | bytes 1324
  0.7 12.5 %copy-start.1 = (f32[128]{0:T(128)S(1)}, f32[128]{0:T(128)}, u32[]{:S(2)}) copy-start(f32[128]{0:T(128)} %param.8) | copy-start | bytes 1540

commit v3 on v2

--- a/solution.py
+++ b/solution.py
@@ -46,13 +46,16 @@
 def kernel(
     n_occ, n_vir, group,
     send_ref, int_ref, screen_ref, row_ref, col_ref, out_ref,
-    recv, ints, acc, parts, red,
-    int_sem, own_sem, send_sems, recv_sems, psend_sems, precv_sems,
+    recv, ints, raw, packed, weights, keeps, acc, parts, red,
+    int_sem, raw_sems, send_sems, recv_sems, psend_sems, precv_sems,
 ):
     n = n_occ * n_vir
     my_occ, my_vir = lax.axis_index("occ"), lax.axis_index("vir")
     me = my_occ * n_vir + my_vir
-    vir_part, rows_here, occ_part = recv.shape[1:]
+    vir_part, rows_here, occ_part = raw.shape[1:]
+    mains, lanes = recv.shape[1], recv.shape[3]
+    extras, spare = vir_part - mains, lanes - occ_part
+    cuts = occ_part // spare
     cols_here, rows_out = red.shape[1:]
 
     tiles_occ, tiles_vir = screen_ref.shape
@@ -71,6 +74,7 @@
 
     load = pltpu.make_async_copy(int_ref, ints, int_sem)
     load.start()
+    slots = raw.shape[0]
 
     bits = n.bit_length() - 1
     order = (0, 3, 4, 1, 2) if bits == 5 else tuple(range(bits))
@@ -86,6 +90,18 @@
         to = partner(step)
         return to // n_vir, lax.rem(to, n_vir)
 
+    def fetch(step):
+        to_occ, to_vir = target(lax.rem(step, n))
+        slot = lax.rem(step, slots)
+        return pltpu.make_async_copy(
+            send_ref.at[to_occ, pl.ds(to_vir * vir_part, vir_part)],
+            raw.at[slot],
+            raw_sems.at[slot],
+        )
+
+    for step in range(1, slots + 1):
+        fetch(step).start()
+
     barrier = pltpu.get_barrier_semaphore()
 
     def greet(step, carry):
@@ -98,7 +114,7 @@
     def block(step):
         to_occ, to_vir = target(step)
         return pltpu.make_async_remote_copy(
-            src_ref=send_ref.at[to_occ, pl.ds(to_vir * vir_part, vir_part)],
+            src_ref=packed.at[step],
             dst_ref=recv.at[step],
             send_sem=send_sems.at[step],
             recv_sem=recv_sems.at[step],
@@ -106,17 +122,57 @@
             device_id_type=MESH,
         )
 
+    def pack(slot, dst, place):
+        def from_extra(e, carry):
+            extra = raw[slot, mains + e].astype(jnp.float32)
+            for g in range(cuts):
+                t = e * cuts + g
+                main = raw[slot, t].astype(jnp.float32)
+                piece_here = extra[:, g * spare:(g + 1) * spare]
+                dst[place, t] = jnp.concatenate([main, piece_here], 1).astype(jnp.bfloat16)
+            return carry
+
+        lax.fori_loop(0, extras, from_extra, 0)
+        for t in range(extras * cuts, mains):
+            main = raw[slot, t].astype(jnp.float32)
+            blank = jnp.zeros((rows_here, spare), jnp.float32)
+            dst[place, t] = jnp.concatenate([main, blank], 1).astype(jnp.bfloat16)
+
     def send_block(step, carry):
+        slot = lax.rem(step, slots)
+        fetch(step).wait()
+        pack(slot, packed, step)
         block(step).start()
+
+        @pl.when(step + slots < n)
+        def _():
+            fetch(step + slots).start()
+
         return carry
 
     lax.fori_loop(1, n, send_block, 0)
-    own = pltpu.make_async_copy(
-        send_ref.at[my_occ, pl.ds(my_vir * vir_part, vir_part)], recv.at[0], own_sem
-    )
-    own.start()
+    fetch(n).start()
+    fetch(n).wait()
+    pack(n % slots, recv, 0)
     load.wait()
-    own.wait()
+
+    def weigh(e, carry):
+        extra = ints[mains + e].astype(jnp.float32)
+        extra_keep = keep(mains + e)
+        for g in range(cuts):
+            t = e * cuts + g
+            part = slice(g * spare, (g + 1) * spare)
+            main = ints[t].astype(jnp.float32)
+            weights[t] = jnp.concatenate([main, extra[part]], 0).astype(jnp.bfloat16)
+            keeps[t] = jnp.concatenate([keep(t), extra_keep[:, part]], 1)
+        return carry
+
+    lax.fori_loop(0, extras, weigh, 0)
+    for t in range(extras * cuts, mains):
+        main = ints[t].astype(jnp.float32)
+        blank = jnp.zeros((spare, main.shape[1]), jnp.float32)
+        weights[t] = jnp.concatenate([main, blank], 0).astype(jnp.bfloat16)
+        keeps[t] = jnp.concatenate([keep(t), jnp.zeros((1, spare), jnp.float32)], 1)
 
     for first in range(0, n, group):
         def arrive(step, carry):
@@ -127,12 +183,12 @@
 
         def multiply(c, total):
             left = recv[first:first + group, c].astype(jnp.float32)
-            left = left.reshape(group * rows_here, occ_part) * keep(c)
+            left = left.reshape(group * rows_here, lanes) * keeps[c]
             left = left.astype(jnp.bfloat16)
-            return total + jnp.dot(left, ints[c], preferred_element_type=jnp.float32)
+            return total + jnp.dot(left, weights[c], preferred_element_type=jnp.float32)
 
         total = lax.fori_loop(
-            0, vir_part, multiply,
+            0, mains, multiply,
             jnp.zeros((group * rows_here, ints.shape[-1]), jnp.float32),
             unroll=4,
         )
@@ -184,6 +240,8 @@
     rows_here, occ_all, vir_all = amplitudes.shape
     occ_part, vir_part, col_total = integrals.shape
     n = n_occ * n_vir
+    lanes = 128
+    mains = vir_part - vir_part // (occ_part // (lanes - occ_part) + 1)
     rows_out, cols_here = row_gap.shape[0], col_gap.shape[0]
     send = jnp.transpose(
         amplitudes.reshape(rows_here, n_occ, occ_part, vir_all), (1, 3, 0, 2)
@@ -200,15 +258,19 @@
         ],
         out_specs=vmem,
         scratch_shapes=[
-            pltpu.VMEM((n, vir_part, rows_here, occ_part), jnp.bfloat16),
+            pltpu.VMEM((n, mains, rows_here, lanes), jnp.bfloat16),
             pltpu.VMEM((vir_part, occ_part, col_total), jnp.bfloat16),
+            pltpu.VMEM((4, vir_part, rows_here, occ_part), jnp.bfloat16),
+            pltpu.VMEM((n, mains, rows_here, lanes), jnp.bfloat16),
+            pltpu.VMEM((mains, lanes, col_total), jnp.bfloat16),
+            pltpu.VMEM((mains, 1, lanes), jnp.float32),
             pltpu.VMEM((n * rows_here, col_total), jnp.float32),
             pltpu.VMEM((n_occ, col_total, rows_out), jnp.float32),
             pltpu.VMEM((n, cols_here, rows_out), jnp.float32),
-            dma, dma, dma((n,)), dma((n,)), dma((n,)), dma((n,)),
+            dma, dma((4,)), dma((n,)), dma((n,)), dma((n,)), dma((n,)),
         ],
         compiler_params=pltpu.CompilerParams(
-            collective_id=0, has_side_effects=True, vmem_limit_bytes=48 * 2**20
+            collective_id=0, has_side_effects=True, vmem_limit_bytes=57 * 2**20
         ),
     )(send, ints, screen, row_gap.reshape(1, rows_out), col_gap.reshape(cols_here, 1))
     return out.T
@@ -223,6 +285,9 @@
             and row_gap.shape[0] % 128 == 0
             and col_gap.shape[0] % 8 == 0
             and (n_occ * n_vir) % 8 == 0
+            and 64 <= integrals.shape[0] < 128
+            and integrals.shape[0] % (128 - integrals.shape[0]) == 0
+            and integrals.shape[0] % 8 == 0
             and (n_occ * n_vir).bit_count() == 1
         )
         if fits:

time: 229 us -> 222 us (0.969)
  Pallas kernels: 215 us -> 206 us
    pallas_call x1, Pallas kernels: 215 us -> 206 us  [kernel_shards(): pl.pallas_call(functools.partial(kernel, n_occ, n_vir, 8), out_shape=jax....]
where the time goes in v3:
time: 222 us; the launch traced here: 221 us
  Pallas kernels  206 us (93%)
  local copies, waits for them, and re-layouts  15.2 us (7%)
    pallas_call x1, Pallas kernels, kernel_shards(): pl.pallas_call(functools.partial(kernel, n_occ, n_vir, 8), out_shape=jax....  206 us
    reshape x1, local copies, waits for them, and re-layouts, kernel_shards(): amplitudes.reshape(rows_here, n_occ, occ_part, vir_all)  12.5 us

profile of v3, /device:TPU:0, one launch (start us, length us, event | category | flops | bytes accessed | tf_op | source)
XLA Modules:
  0.0 221.2 jit_solution(3612488925934744222)
XLA Ops:
  0.0 1.3 copy.8.col_ref
  1.3 12.5 %copy.7 = bf16[8,2,120,2112]{2,0,3,1:T(8,128)(2,1)} copy(bf16[8,2,120,2112]{3,2,1,0:T(8,128)(2,1)} %bitcast.7) | data formatting | bytes 16220160 | tf_op jit(solution)/shard_map/reshape | solution.py:247
  13.9 206.0 %shard_map.55 = f32[16,128]{1,0:T(8,128)} custom-call(bf16[2,2112,8,120]{3,2,1,0:T(8,128)(2,1)} %bitcast.6, bf16[132,120,256]{2,1,0:T(8,128)(2,1)} %bitcast.8, s32[5,22]{1,0:T(8,128)} %screen_ref.1, f32[1,128]{1,0:T(1,128)} %bitcast.10, f32[16,1]{1,0:T(8,128)} %copy.8.col_ref), custom_call_target="tpu_custom_call" | custom-call | tf_op jit(solution)/shard_map/pallas_call | solution.py:253
  219.9 1.3 copy.10

commit v4 on v3

--- a/solution.py
+++ b/solution.py
@@ -77,7 +77,7 @@
     slots = raw.shape[0]
 
     bits = n.bit_length() - 1
-    order = (0, 3, 4, 1, 2) if bits == 5 else tuple(range(bits))
+    order = (0, 3, 1, 4, 2) if bits == 5 else tuple(range(bits))
 
     def partner(step):
         to = me
@@ -190,7 +190,7 @@
         total = lax.fori_loop(
             0, mains, multiply,
             jnp.zeros((group * rows_here, ints.shape[-1]), jnp.float32),
-            unroll=4,
+            unroll=31,
         )
         for place in range(group):
             origin = partner(first + place)

time: 222 us -> 215 us (0.968)
  Pallas kernels: 206 us -> 199 us
    pallas_call x1, Pallas kernels: 206 us -> 199 us  [kernel_shards(): pl.pallas_call(functools.partial(kernel, n_occ, n_vir, 8), out_shape=jax....]
where the time goes in v4:
time: 215 us; the launch traced here: 214 us
  Pallas kernels  199 us (93%)
  local copies, waits for them, and re-layouts  15.2 us (7%)
    pallas_call x1, Pallas kernels, kernel_shards(): pl.pallas_call(functools.partial(kernel, n_occ, n_vir, 8), out_shape=jax....  199 us
    reshape x1, local copies, waits for them, and re-layouts, kernel_shards(): amplitudes.reshape(rows_here, n_occ, occ_part, vir_all)  12.5 us

profile of v4, /device:TPU:0, one launch (start us, length us, event | category | flops | bytes accessed | tf_op | source)
XLA Modules:
  0.0 214.3 jit_solution(394805101494980839)
XLA Ops:
  0.0 1.3 copy.8.col_ref
  1.3 12.5 %copy.7 = bf16[8,2,120,2112]{2,0,3,1:T(8,128)(2,1)} copy(bf16[8,2,120,2112]{3,2,1,0:T(8,128)(2,1)} %bitcast.7) | data formatting | bytes 16220160 | tf_op jit(solution)/shard_map/reshape | solution.py:247
  13.9 199.2 %shard_map.55 = f32[16,128]{1,0:T(8,128)} custom-call(bf16[2,2112,8,120]{3,2,1,0:T(8,128)(2,1)} %bitcast.6, bf16[132,120,256]{2,1,0:T(8,128)(2,1)} %bitcast.8, s32[5,22]{1,0:T(8,128)} %screen_ref.1, f32[1,128]{1,0:T(1,128)} %bitcast.10, f32[16,1]{1,0:T(8,128)} %copy.8.col_ref), custom_call_target="tpu_custom_call" | custom-call | tf_op jit(solution)/shard_map/pallas_call | solution.py:253
  213.0 1.3 copy.10

commit v5 on v4

--- a/solution.py
+++ b/solution.py
@@ -77,7 +77,7 @@
     slots = raw.shape[0]
 
     bits = n.bit_length() - 1
-    order = (0, 3, 1, 4, 2) if bits == 5 else tuple(range(bits))
+    order = (0, 1, 3, 4, 2) if bits == 5 else tuple(range(bits))
 
     def partner(step):
         to = me

time: 215 us -> 217 us (level)
  no operation moved by 1% of the time
where the time goes in v5:
time: 217 us; the launch traced here: 216 us
  Pallas kernels  201 us (93%)
  local copies, waits for them, and re-layouts  15.2 us (7%)
    pallas_call x1, Pallas kernels, kernel_shards(): pl.pallas_call(functools.partial(kernel, n_occ, n_vir, 8), out_shape=jax....  201 us
    reshape x1, local copies, waits for them, and re-layouts, kernel_shards(): amplitudes.reshape(rows_here, n_occ, occ_part, vir_all)  12.5 us

profile of v5, /device:TPU:0, one launch (start us, length us, event | category | flops | bytes accessed | tf_op | source)
XLA Modules:
  0.0 216.1 jit_solution(448648137848624704)
XLA Ops:
  0.0 1.3 copy.8.col_ref
  1.3 12.5 %copy.7 = bf16[8,2,120,2112]{2,0,3,1:T(8,128)(2,1)} copy(bf16[8,2,120,2112]{3,2,1,0:T(8,128)(2,1)} %bitcast.7) | data formatting | bytes 16220160 | tf_op jit(solution)/shard_map/reshape | solution.py:247
  13.9 200.9 %shard_map.55 = f32[16,128]{1,0:T(8,128)} custom-call(bf16[2,2112,8,120]{3,2,1,0:T(8,128)(2,1)} %bitcast.6, bf16[132,120,256]{2,1,0:T(8,128)(2,1)} %bitcast.8, s32[5,22]{1,0:T(8,128)} %screen_ref.1, f32[1,128]{1,0:T(1,128)} %bitcast.10, f32[16,1]{1,0:T(8,128)} %copy.8.col_ref), custom_call_target="tpu_custom_call" | custom-call | tf_op jit(solution)/shard_map/pallas_call | solution.py:253
  214.8 1.3 copy.10
